TPU v7x, 32 devices: a whole 2x2x4 slice. The times are simulated.
32 devices in a mesh: dp: 4 (over y, x), ctx: 8 (over z, core).
Axes of the slice: x: 2, y: 2, z: 4, core: 2. Of those that a mesh axis runs over, the one named last changes fastest.
Arguments:
- inputs: bfloat16 [8192, 8192], P(('dp', 'ctx')), parts along dimension 0, may hold values from -6 to 6
- key_query: bfloat16 [8192, 2048], P(('dp', 'ctx')), parts along dimension 0, may hold values from -3 to 3
- conv_inputs: float32 [4, 8192], replicated, may hold values from -3 to 3
- conv_kq: float32 [4, 2048], replicated, may hold values from -3 to 3
- step_size: float32 [8192, 128], P(('dp', 'ctx')), parts along dimension 0, may hold values from 0.1 to 1
- decay_log: float32 [8192, 128], P(('dp', 'ctx')), parts along dimension 0, may hold values from -1 to 0, as said below
- skip_gain: float32 [128], replicated, may hold values from 0.5 to 1.5
- norm_gain: float32 [8192], replicated, may hold values from 0.5 to 1.5
Outputs:
- mixed: bfloat16 [8192, 8192], P('dp', 'ctx'), parts along dimension 0
There are 4 independent parts, one for each index of `dp`. A program takes and returns all parts, laid end to end along the dimension named above; an argument that names none is the same for every part. Nothing has to cross between parts.
Inputs may be any that keep to these rules, and one draw needn't show every extreme that they name: `decay_log`: log decay factors, all negative.
All inputs are finite; a program needn't handle non-finite values.
Results may differ from a plain program's by a relative error of at most 0.0085.
Values may be sent and summed in bfloat16 or wider, within the bound.
No kernel may reach another device: no remote copies, remote signals or barrier semaphores. Data moves between devices by JAX's collectives and lax.ppermute only.
A program may use at most 448 MiB of HBM per device.

v0:
```python
import functools

import jax
import jax.numpy as jnp
from jax import lax
from jax.experimental import pallas as pl
from jax.experimental.pallas import tpu as pltpu
from jax.sharding import PartitionSpec as P

HEADS = 128
HEAD_DIM = 64
STATE = 128
GROUPS = 8
KW = 4
BLOCK = 128
GROUP_WIDTH = HEADS * HEAD_DIM // GROUPS
EPS = 1e-05
HALO = 16
LANES = 128
SUBLANES = 8
FIELDS = 2
STRIP = 64
PAIR = 2
WINDOW = 5
ORDER = (1, 7, 4, 3, 5, 2, 6)
ARRIVAL = (1, 7, 2, 6, 4, 3, 5)
PACK_VMEM = 58 * 1024 * 1024
VMEM_LIMIT = 28 * 1024 * 1024


def contract(a, b, dims):
    return lax.dot_general(a, b, (dims, ((), ())), preferred_element_type=jnp.float32)


def as_parts(v, count):
    parts = []
    for _ in range(count):
        part = v.astype(jnp.bfloat16)
        parts.append(part)
        v = v - part.astype(jnp.float32)
    return parts


def scalar_units(heads, rows, cols):
    units = []
    for p in range(FIELDS):
        for head in range(0, heads, SUBLANES):
            line, column = divmod(len(units), cols // rows)
            units.append((p, head, min(SUBLANES, heads), line * SUBLANES, column * rows))
    return units


def pack_kernel(peers, span, width, heads, codes, *refs):
    owner_ref, x_ref, kq_ref, decay_ref, step_ref = refs[:5]
    outs = refs[5 : 5 + len(codes)]
    raw_scalars, scalars, kq_near, sems = refs[5 + len(codes) :]
    rows = x_ref.shape[0]
    copies = [
        pltpu.make_async_copy(ref, dst, sems.at[1, i])
        for i, (ref, dst) in enumerate(
            ((decay_ref, raw_scalars.at[0]), (step_ref, raw_scalars.at[1]), (kq_ref, kq_near))
        )
    ]
    owners = [owner_ref[code] for code in codes]
    for i, owner in enumerate(owners):
        column = pl.multiple_of(owner * width, LANES)
        copies.append(
            pltpu.make_async_copy(
                x_ref.at[:, pl.ds(column, width)], outs[i].at[0:rows, 0:width], sems.at[0, i]
            )
        )
    for copy in copies:
        copy.start()
    for copy in copies[:3]:
        copy.wait()
    for p in range(FIELDS):
        field = raw_scalars[p].T
        for owner in range(peers):
            scalars[p, owner] = field[owner * heads : (owner + 1) * heads]
    for i, owner in enumerate(owners):
        outs[i][rows:] = jnp.zeros((outs[i].shape[0] - rows, outs[i].shape[1]), jnp.bfloat16)
        for p, head, count, top, left in scalar_units(heads, rows, width + 2 * STATE):
            outs[i][rows + top : rows + top + count, left : left + rows] = scalars[
                p, owner, head : head + count
            ].astype(jnp.bfloat16)
        for j in range(2):
            column = pl.multiple_of((j * GROUPS + owner // span) * STATE, LANES)
            left = width + j * STATE
            outs[i][0:rows, left : left + STATE] = kq_near[:, pl.ds(column, STATE)]
    for copy in copies[3:]:
        copy.wait()


def spread(heads):
    head_of = lax.broadcasted_iota(jnp.int32, (2 * heads, heads * HEAD_DIM), 1) // HEAD_DIM
    row = lax.rem(lax.broadcasted_iota(jnp.int32, (2 * heads, heads * HEAD_DIM), 0), heads)
    return jnp.where(head_of == row, 1.0, 0.0).astype(jnp.bfloat16)


def local_kernel(width, heads, count, chained, *refs):
    source_ref = refs[0]
    parts = refs[1 : 1 + 2 * count]
    taps_ref, skip_ref = refs[1 + 2 * count : 3 + 2 * count]
    refs = refs[3 + 2 * count + (5 if chained else 0) :]
    pre, state, c_out, fade_out, edge_out = refs[:5]
    wide, x_ref, scaled_ref, scales = refs[5:]
    rows = x_ref.shape[0]
    blocks = rows // BLOCK
    full = width + 2 * STATE
    row = lax.broadcasted_iota(jnp.int32, (rows, rows), 0)
    col = lax.broadcasted_iota(jnp.int32, (rows, rows), 1)
    lower = (row >= col) & (row // BLOCK == col // BLOCK)
    ones = jnp.where(lower, 1.0, 0.0).astype(jnp.bfloat16)
    eye = jnp.where(row == col, 1.0, 0.0).astype(jnp.bfloat16)
    expand = spread(heads)

    for which in range(count):
        source = source_ref[which]
        part, earlier = parts[2 * which : 2 * which + 2]
        wide[HALO:] = part[0:rows, 0:full]
        edge = earlier[rows - HALO : rows, 0:full]
        wide[0:HALO] = jnp.where(source == 0, jnp.zeros_like(edge), edge)

        def activated(r, lane):
            tap = [taps_ref[k : k + 1, lane : lane + LANES] for k in range(KW)]
            now = wide[r : r + STRIP + HALO, lane : lane + LANES].astype(jnp.float32)
            now = now[HALO // 2 :]
            before = pltpu.roll(now, 1, 0)
            older = pltpu.roll(tap[0] * before + tap[1] * now, 2, 0)
            summed = (older + (tap[2] * before + tap[3] * now))[HALO // 2 :]
            return summed * pltpu.reciprocal(1.0 + jnp.exp(-summed), approx=True)

        def field(p):
            pieces = [
                part[rows + top : rows + top + size, left : left + rows].astype(jnp.float32)
                for q, _, size, top, left in scalar_units(heads, rows, full)
                if q == p
            ]
            return jnp.concatenate(pieces, axis=0).astype(jnp.bfloat16)

        cumul = contract(ones, field(0), ((1,), (1,)))
        steps = contract(eye, field(1), ((1,), (1,)))
        middles = [
            cumul[b * BLOCK + BLOCK // 2 - 1 : b * BLOCK + BLOCK // 2] for b in range(blocks)
        ]
        middle = jnp.concatenate([jnp.broadcast_to(m, (BLOCK, heads)) for m in middles], axis=0)
        inward = jnp.concatenate(as_parts(steps * jnp.exp(middle - cumul), 2), axis=1)
        outward = jnp.concatenate(
            as_parts(
                jnp.concatenate(
                    [jnp.exp(cumul - middle)]
                    + [jnp.broadcast_to(jnp.exp(m), (16, heads)) for m in middles],
                    axis=0,
                ),
                2,
            ),
            axis=1,
        )
        scales[...] = contract(
            jnp.concatenate([inward, outward], axis=0), expand, ((1,), (0,))
        )
        edges = []
        for b in range(blocks):
            last_row = rows + (b + 1) * BLOCK - 1
            middle_row = 2 * rows + 16 * b
            edges += [scales[middle_row : middle_row + 1], scales[last_row : last_row + 1]]
        edge_out[source, 0 : 2 * blocks] = jnp.concatenate(edges, axis=0)
        fade_out[source] = scales[rows : 2 * rows].astype(jnp.bfloat16)
        b_part, c_part = (
            jnp.concatenate(
                [activated(r, lane) for r in range(0, rows, STRIP)], axis=0
            ).astype(jnp.bfloat16)
            for lane in (width, width + STATE)
        )
        c_out[source] = c_part
        scores = contract(c_part, b_part, ((1,), (1,)))
        scores = jnp.where(lower, scores, 0.0).astype(jnp.bfloat16)
        for lane in range(0, width, LANES):
            at = slice(lane, lane + LANES)
            for r in range(0, rows, STRIP):
                x_conv = activated(r, lane)
                x_ref[r : r + STRIP, at] = x_conv
                scaled_ref[r : r + STRIP, at] = (x_conv * scales[r : r + STRIP, at]).astype(
                    jnp.bfloat16
                )
        for b in range(blocks):
            at = slice(b * BLOCK, (b + 1) * BLOCK)
            added = contract(b_part[at], scaled_ref[at], ((0,), (0,)))
            state[source, b * STATE : (b + 1) * STATE] = added.astype(jnp.bfloat16)
        intra = contract(scores, scaled_ref[...], ((1,), (0,)))
        pre[source] = (intra * scales[rows : 2 * rows] + skip_ref[...] * x_ref[...]).astype(jnp.bfloat16)


def carry_kernel(width, whole_group, *refs):
    pre, state, c_part, fade, edge, gain_ref = refs[:6]
    outs, carry = refs[6:-1], refs[-1]
    rows = pre.shape[1]
    blocks = rows // BLOCK
    step = pl.program_id(0)

    @pl.when(step == 0)
    def _():
        carry[...] = jnp.zeros_like(carry)

    held = []
    for half in range(PAIR):
        source = step * PAIR + half
        for b in range(blocks):
            now = carry[...] * edge[source, 2 * b : 2 * b + 1]
            held.append(now.astype(jnp.bfloat16))
            added = state[source, b * STATE : (b + 1) * STATE].astype(jnp.float32)
            carry[...] = (now + added) * edge[source, 2 * b + 1 : 2 * b + 2]
    for half in range(PAIR):
        source = step * PAIR + half
        for b in range(blocks):
            at = slice(b * BLOCK, (b + 1) * BLOCK)
            to = slice(half * rows + b * BLOCK, half * rows + (b + 1) * BLOCK)
            inter = contract(c_part[source, at], held[half * blocks + b], ((1,), (0,)))
            total = pre[source, at].astype(jnp.float32) + inter * fade[source, at].astype(
                jnp.float32
            )
            power = total[:, :LANES] * total[:, :LANES]
            for lane in range(LANES, width, LANES):
                power = power + total[:, lane : lane + LANES] * total[:, lane : lane + LANES]
            if whole_group:
                summed = jnp.sum(power, axis=1, keepdims=True)
                norm = lax.rsqrt(summed * (1.0 / GROUP_WIDTH) + EPS)
                outs[0][to] = (total * norm * gain_ref[...]).astype(jnp.bfloat16)
            else:
                outs[0][to] = total
                outs[1][to] = power


def per_device(inputs, key_query, conv_inputs, conv_kq, step_size, decay_log, skip_gain, norm_gain):
    peers = lax.axis_size("ctx")
    me = lax.axis_index("ctx")
    rows = inputs.shape[0]
    width = HEADS * HEAD_DIM // peers
    heads = HEADS // peers
    span = GROUP_WIDTH // width
    whole_group = span == 1
    blocks = rows // BLOCK
    full = width + 2 * STATE
    scalar_rows = scalar_units(heads, rows, full)[-1][3] + SUBLANES
    scale_rows = rows + 16 * blocks
    cycle = jnp.arange(peers, dtype=jnp.int32)
    owners = lax.rem(me + cycle, peers)
    sources = lax.rem(me + peers - cycle, peers)

    smem = pl.BlockSpec(memory_space=pltpu.SMEM)
    hbm = pl.BlockSpec(memory_space=pltpu.HBM)
    vmem = pl.BlockSpec(memory_space=pltpu.VMEM)
    params = pltpu.CompilerParams(vmem_limit_bytes=VMEM_LIMIT)

    def columns(a, first, size):
        return lax.dynamic_slice_in_dim(a, first, size, axis=1)

    def pack(codes):
        shape = jax.ShapeDtypeStruct((rows + scalar_rows, full), jnp.bfloat16)
        return pl.pallas_call(
            functools.partial(pack_kernel, peers, span, width, heads, codes),
            in_specs=[smem] + [hbm] * 4,
            out_specs=[vmem] * len(codes),
            out_shape=[shape] * len(codes),
            scratch_shapes=[
                pltpu.VMEM((FIELDS, rows, HEADS), jnp.float32),
                pltpu.VMEM((FIELDS, peers, heads, rows), jnp.float32),
                pltpu.VMEM(key_query.shape, jnp.bfloat16),
                pltpu.SemaphoreType.DMA((2, max(3, len(codes)))),
            ],
            compiler_params=pltpu.CompilerParams(vmem_limit_bytes=PACK_VMEM),
            cost_estimate=pl.CostEstimate(
                flops=0, bytes_accessed=4 * len(codes) * rows * full, transcendentals=0
            ),
            name="pack",
        )(owners, inputs, key_query, decay_log, step_size)

    codes = [code for code in ORDER if code < peers]
    codes += [code for code in range(1, peers) if code not in codes]
    parts = dict(zip(codes[:WINDOW], pack(codes[:WINDOW])))
    parts.update(zip(codes[WINDOW:] + [0], pack(codes[WINDOW:] + [0])))
    for i, code in enumerate(codes):
        pairs = [(j, (j + code) % peers) for j in range(peers)]
        message = parts[code]
        if i >= WINDOW:
            message, _ = lax.optimization_barrier((message, parts[codes[i - WINDOW]]))
        parts[code] = lax.ppermute(message, "ctx", pairs)

    group = me // span
    taps = jnp.concatenate(
        [
            columns(conv_inputs, me * width, width),
            columns(conv_kq, group * STATE, STATE),
            columns(conv_kq, (GROUPS + group) * STATE, STATE),
        ],
        axis=1,
    )
    skip = jnp.repeat(lax.dynamic_slice_in_dim(skip_gain, me * heads, heads), HEAD_DIM)[None]
    gain = columns(norm_gain[None], me * width, width)

    shapes = [
        ((rows, width), jnp.bfloat16),
        ((blocks * STATE, width), jnp.bfloat16),
        ((rows, STATE), jnp.bfloat16),
        ((rows, width), jnp.bfloat16),
        ((2 * blocks, width), jnp.float32),
    ]
    codes_after = tuple(code for code in codes if code not in ARRIVAL)
    arrived = {0}
    pending = list(range(peers))
    stores = []
    for code in sorted(codes, key=lambda code: (ARRIVAL + codes_after).index(code)):
        arrived.add(code)
        ready = [k for k in pending if {k, (k + 1) % peers} <= arrived]
        pending = [k for k in pending if k not in ready]
        if not ready:
            continue
        count = len(ready)
        operands = []
        for k in ready:
            operands += [parts[k], parts[(k + 1) % peers]]
        stores = pl.pallas_call(
            functools.partial(local_kernel, width, heads, count, bool(stores)),
            in_specs=[smem] + [vmem] * (2 * count + 2 + len(stores)),
            out_specs=[vmem] * len(shapes),
            out_shape=[jax.ShapeDtypeStruct((peers,) + shape, dtype) for shape, dtype in shapes],
            input_output_aliases={3 + 2 * count + i: i for i in range(len(stores))},
            scratch_shapes=[
                pltpu.VMEM((rows + HALO, full), jnp.bfloat16),
                pltpu.VMEM((rows, width), jnp.float32),
                pltpu.VMEM((rows, width), jnp.bfloat16),
                pltpu.VMEM((rows + scale_rows, width), jnp.float32),
            ],
            compiler_params=params,
            cost_estimate=pl.CostEstimate(
                flops=2 * rows * count * width * 450,
                bytes_accessed=count * rows * width * 10,
                transcendentals=count * rows * full,
            ),
            name="local",
        )(jnp.stack([sources[k] for k in ready]), *operands, taps, skip, *stores)

    out = [((rows, width), jnp.bfloat16 if whole_group else jnp.float32)]
    if not whole_group:
        out.append(((rows, LANES), jnp.float32))
    results = pl.pallas_call(
        functools.partial(carry_kernel, width, whole_group),
        grid=(peers // PAIR,),
        in_specs=[vmem] * (len(shapes) + 1),
        out_specs=[pl.BlockSpec((PAIR * shape[0], shape[1]), lambda i: (i, 0)) for shape, _ in out],
        out_shape=[
            jax.ShapeDtypeStruct((peers * shape[0], shape[1]), dtype) for shape, dtype in out
        ],
        scratch_shapes=[
            pltpu.VMEM((STATE, width), jnp.float32),
        ],
        compiler_params=params,
        cost_estimate=pl.CostEstimate(
            flops=2 * peers * rows * width * 150,
            bytes_accessed=peers * rows * width * 8,
            transcendentals=peers * rows,
        ),
        name="carry",
    )(*stores, gain)
    if whole_group:
        return results[0]
    total, power = results
    sharers = [list(range(i, i + span)) for i in range(0, peers, span)]
    summed = jnp.sum(power, axis=1, keepdims=True)
    summed = lax.psum(summed, "ctx", axis_index_groups=sharers)
    return (total * lax.rsqrt(summed * (1.0 / GROUP_WIDTH) + EPS) * gain).astype(jnp.bfloat16)


def solution(mesh):
    in_specs = (
        P(("dp", "ctx"), None),
        P(("dp", "ctx"), None),
        P(),
        P(),
        P(("dp", "ctx"), None),
        P(("dp", "ctx"), None),
        P(),
        P(),
    )
    out_specs = P("dp", "ctx")
    return jax.shard_map(
        per_device, mesh=mesh, in_specs=in_specs, out_specs=out_specs, check_vma=False
    )
```

profile of v0, /device:TPU:12, one launch (start us, length us, event | category | flops | bytes accessed | tf_op | source)
XLA Modules:
  0.0 143.3 jit_solution(5451859833111629647)
XLA Ops:
  0.0 0.0 copy-start
  0.0 0.6 compare_select_fusion.refs_0_
  0.6 0.0 copy-start.5
  0.6 4.8 %pack.2 = (bf16[264,1280]{1,0:T(8,128)(2,1)}, bf16[264,1280]{1,0:T(8,128)(2,1)}, bf16[264,1280]{1,0:T(8,128)(2,1)}, bf16[264,1280]{1,0:T(8,128)(2,1)}, bf16[264,1280]{1,0:T(8,128)(2,1)}) custom-call(s32[8]{0:T(128)} %compare_select_fusion.refs_0_, bf16[256,8192]{1,0:T(8,128)(2,1)} %refs_1_.3, bf16[256,2048]{1,0:T(8,128)(2,1)} %refs_2_.3, ...), custom_call_target="tpu_custom_call" | custom-call | bytes 6553600 | tf_op jit(solution)/shard_map/pack/pallas_call | solution.py:260
  5.4 0.1 collective-permute-start.4
  5.4 1.7 %collective-permute-start.2 = (bf16[264,1280]{1,0:T(8,128)(2,1)}, bf16[264,1280]{1,0:T(8,128)(2,1)S(1)}, u32[]{:S(2)}, u32[]{:S(2)}) collective-permute-start(bf16[264,1280]{1,0:T(8,128)(2,1)} %get-tuple-element.48), channel_id=1, source_target_pairs={{0,7},{1,0},{2,1},{3,2},{4,3},{5,4},{6,5},{7,6},{8,15},{9,8},{10,9... | collective-permute-start | bytes 2027528 | tf_op jit(solution)/shard_map/ppermute | solution.py:287
  7.2 2.6 %collective-permute-start = (bf16[264,1280]{1,0:T(8,128)(2,1)}, bf16[264,1280]{1,0:T(8,128)(2,1)S(1)}, u32[]{:S(2)}, u32[]{:S(2)}) collective-permute-start(bf16[264,1280]{1,0:T(8,128)(2,1)} %get-tuple-element.45), channel_id=1, source_target_pairs={{0,4},{1,5},{2,6},{3,7},{4,0},{5,1},{6,2},{7,3},{8,12},{9,13},{10,... | collective-permute-start | bytes 2027528 | tf_op jit(solution)/shard_map/ppermute | solution.py:287
  9.8 0.0 collective-permute-start.6
  9.8 2.6 %collective-permute-start.1 = (bf16[264,1280]{1,0:T(8,128)(2,1)}, bf16[264,1280]{1,0:T(8,128)(2,1)S(1)}, u32[]{:S(2)}, u32[]{:S(2)}) collective-permute-start(bf16[264,1280]{1,0:T(8,128)(2,1)} %get-tuple-element.46), channel_id=1, source_target_pairs={{0,5},{1,6},{2,7},{3,0},{4,1},{5,2},{6,3},{7,4},{8,13},{9,14},{10,... | collective-permute-start | bytes 2027528 | tf_op jit(solution)/shard_map/ppermute | solution.py:287
  12.4 3.9 %pack.3 = (bf16[264,1280]{1,0:T(8,128)(2,1)}, bf16[264,1280]{1,0:T(8,128)(2,1)}, bf16[264,1280]{1,0:T(8,128)(2,1)}) custom-call(s32[8]{0:T(128)} %compare_select_fusion.refs_0_, bf16[256,8192]{1,0:T(8,128)(2,1)} %refs_1_.3, bf16[256,2048]{1,0:T(8,128)(2,1)} %refs_2_.3, f32[256,128]{1,0:T(8,128)} %refs_3_.3, f32[256,128]{1,0:T(8,128)} %refs_4_.3), custom_call_target="tpu_custom_call" | custom-call | bytes 3932160 | tf_op jit(solution)/shard_map/pack/pallas_call | solution.py:260
  16.3 0.0 copy-done
  16.3 4.2 %collective-permute-done.4.refs_2_.refs_1_ = bf16[264,1280]{1,0:T(8,128)(2,1)S(1)} collective-permute-done((bf16[264,1280]{1,0:T(8,128)(2,1)}, bf16[264,1280]{1,0:T(8,128)(2,1)S(1)}, u32[]{:S(2)}, u32[]{:S(2)}) %collective-permute-start.4) | collective-permute-done | bytes 675872 | tf_op jit(solution)/shard_map/ppermute | solution.py:287
  20.5 0.0 copy-start.1
  20.5 0.8 copy-done.1
  21.3 29.9 %collective-permute-start.5 = (bf16[264,1280]{1,0:T(8,128)(2,1)}, bf16[264,1280]{1,0:T(8,128)(2,1)}, u32[]{:S(2)}, u32[]{:S(2)}) collective-permute-start(bf16[264,1280]{1,0:T(8,128)(2,1)} %get-tuple-element.52), channel_id=1, source_target_pairs={{0,2},{1,3},{2,4},{3,5},{4,6},{5,7},{6,0},{7,1},{8,10},{9,11},{10,... | collective-permute-start | bytes 2027528 | tf_op jit(solution)/shard_map/ppermute | solution.py:287
  51.2 0.0 collective-permute-done.2.refs_1_.refs_2_
  51.2 0.0 collective-permute-start.3
  51.2 0.7 fusion.2
  51.9 0.0 copy-done.5
  51.9 0.1 dynamic_slice.18
  51.9 0.1 broadcast_in_dim.4
  52.0 0.1 broadcast_in_dim_reshape.3.refs_4_.refs_6_
  52.1 0.7 dynamic-slice.3
  52.8 0.7 constant_dynamic-slice_fusion.1
  53.5 0.1 fusion.3
  53.6 0.0 copy-start.2
  53.6 1.1 copy-done.2
  54.6 0.0 copy-start.4
  54.7 1.1 copy-done.4
  55.7 2.3 %local.6 = (bf16[8,256,1024]{2,1,0:T(8,128)(2,1)S(1)}, bf16[8,256,1024]{2,1,0:T(8,128)(2,1)S(1)}, bf16[8,256,128]{2,1,0:T(8,128)(2,1)S(1)}, bf16[8,256,1024]{2,1,0:T(8,128)(2,1)S(1)}, f32[8,4,1024]{2,1,0:T(4,128)S(1)}) custom-call(s32[1]{0:T(128)} %get-tuple-element.87.refs_0_, bf16[264,1280]{1,0:T(8,128)(2,1)S(1)} %copy-done.4, ...), custom_call_target="tpu_custom_call" | custom-call | flops 235929600 | bytes 2621440 | tf_op jit(solution)/shard_map/local/pallas_call | solution.py:322
  58.1 0.0 copy-start.3
  58.1 2.4 %local.7 = (bf16[8,256,1024]{2,1,0:T(8,128)(2,1)S(1)}, bf16[8,256,1024]{2,1,0:T(8,128)(2,1)S(1)}, bf16[8,256,128]{2,1,0:T(8,128)(2,1)S(1)}, bf16[8,256,1024]{2,1,0:T(8,128)(2,1)S(1)}, f32[8,4,1024]{2,1,0:T(4,128)S(1)}) custom-call(s32[1]{0:T(128)} %get-tuple-element.88.refs_0_, ...), custom_call_target="tpu_custom_call", output_to_operand_aliasing={{0}: (5, {}), {1}: (6, {}), {2}: (7, {}), {3}: (8, {}), {4}... | custom-call | flops 235929600 | bytes 2621440 | tf_op jit(solution)/shard_map/local/pallas_call | solution.py:322
  60.5 63.3 %collective-permute-done.5.refs_2_.refs_1_ = bf16[264,1280]{1,0:T(8,128)(2,1)} collective-permute-done((bf16[264,1280]{1,0:T(8,128)(2,1)}, bf16[264,1280]{1,0:T(8,128)(2,1)}, u32[]{:S(2)}, u32[]{:S(2)}) %collective-permute-start.5) | collective-permute-done | bytes 675872 | tf_op jit(solution)/shard_map/ppermute | solution.py:287
  123.7 0.0 copy-done.3
  123.7 3.4 %local.8 = (bf16[8,256,1024]{2,1,0:T(8,128)(2,1)S(1)}, bf16[8,256,1024]{2,1,0:T(8,128)(2,1)S(1)}, bf16[8,256,128]{2,1,0:T(8,128)(2,1)S(1)}, bf16[8,256,1024]{2,1,0:T(8,128)(2,1)S(1)}, f32[8,4,1024]{2,1,0:T(4,128)S(1)}) custom-call(s32[1]{0:T(128)} %get-tuple-element.89.refs_0_, ...), custom_call_target="tpu_custom_call", output_to_operand_aliasing={{0}: (5, {}), {1}: (6, {}), {2}: (7, {}), {3}: (8, {}), {4}... | custom-call | flops 235929600 | bytes 2621440 | tf_op jit(solution)/shard_map/local/pallas_call | solution.py:322
  127.1 0.0 collective-permute-done.3.refs_1_.refs_4_
  127.2 2.3 %local.9 = (bf16[8,256,1024]{2,1,0:T(8,128)(2,1)S(1)}, bf16[8,256,1024]{2,1,0:T(8,128)(2,1)S(1)}, bf16[8,256,128]{2,1,0:T(8,128)(2,1)S(1)}, bf16[8,256,1024]{2,1,0:T(8,128)(2,1)S(1)}, f32[8,4,1024]{2,1,0:T(4,128)S(1)}) custom-call(s32[1]{0:T(128)} %get-tuple-element.90.refs_0_, ...), custom_call_target="tpu_custom_call", output_to_operand_aliasing={{0}: (5, {}), {1}: (6, {}), {2}: (7, {}), {3}: (8, {}), {4}... | custom-call | flops 235929600 | bytes 2621440 | tf_op jit(solution)/shard_map/local/pallas_call | solution.py:322
  129.5 0.0 collective-permute-done.refs_4_.refs_1_
  129.5 0.0 collective-permute-done.6.refs_2_.refs_3_
  129.5 4.5 %local.10 = (bf16[8,256,1024]{2,1,0:T(8,128)(2,1)S(1)}, bf16[8,256,1024]{2,1,0:T(8,128)(2,1)S(1)}, bf16[8,256,128]{2,1,0:T(8,128)(2,1)S(1)}, bf16[8,256,1024]{2,1,0:T(8,128)(2,1)S(1)}, f32[8,4,1024]{2,1,0:T(4,128)S(1)}) custom-call(s32[2]{0:T(128)S(1)} %get-tuple-element.91.refs_0_, ...), custom_call_target="tpu_custom_call", output_to_operand_aliasing={{0}: (7, {}), {1}: (8, {}), {2}: (9, {}), {3}: (10, {}), {4... | custom-call | flops 471859200 | bytes 5242880 | tf_op jit(solution)/shard_map/local/pallas_call | solution.py:322
  134.0 0.0 collective-permute-done.1.refs_2_.refs_3_
  134.0 3.9 %local.11 = (bf16[8,256,1024]{2,1,0:T(8,128)(2,1)S(1)}, bf16[8,256,1024]{2,1,0:T(8,128)(2,1)S(1)}, bf16[8,256,128]{2,1,0:T(8,128)(2,1)S(1)}, bf16[8,256,1024]{2,1,0:T(8,128)(2,1)S(1)}, f32[8,4,1024]{2,1,0:T(4,128)S(1)}) custom-call(s32[2]{0:T(128)S(1)} %get-tuple-element.92.refs_0_, ...), custom_call_target="tpu_custom_call", output_to_operand_aliasing={{0}: (7, {}), {1}: (8, {}), {2}: (9, {}), {3}: (10, {}), {4... | custom-call | flops 471859200 | bytes 5242880 | tf_op jit(solution)/shard_map/local/pallas_call | solution.py:322
  137.8 5.4 %carry.1 = bf16[2048,1024]{1,0:T(8,128)(2,1)} custom-call(bf16[8,256,1024]{2,1,0:T(8,128)(2,1)S(1)} %get-tuple-element.80.refs_0_, bf16[8,256,1024]{2,1,0:T(8,128)(2,1)S(1)} %get-tuple-element.81.refs_1_, bf16[8,256,128]{2,1,0:T(8,128)(2,1)S(1)} %get-tuple-element.82.refs_2_, bf16[8,256,1024]{2,1,0:T(8,128)(2,1)S(1)} %get-tuple-element.83.refs_3_, ...), custom_call_target="tpu_custom_call" | custom-call | flops 629145600 | bytes 16777216 | tf_op jit(solution)/shard_map/carry/pallas_call | solution.py:346
  (3 shorter events, 0.0 us)
Async XLA Ops:
  0.0 16.3 %copy-start = (f32[4,8192]{1,0:T(4,128)S(1)}, f32[4,8192]{1,0:T(4,128)}, u32[]{:S(2)}) copy-start(f32[4,8192]{1,0:T(4,128)} %param.10) | copy-start | bytes 393220
  0.6 51.3 %copy-start.5 = (f32[128]{0:T(128)S(1)}, f32[128]{0:T(128)}, u32[]{:S(2)}) copy-start(f32[128]{0:T(128)} %param.14) | copy-start | bytes 1540
  5.4 15.1 %collective-permute-start.4 = (bf16[264,1280]{1,0:T(8,128)(2,1)}, bf16[264,1280]{1,0:T(8,128)(2,1)S(1)}, u32[]{:S(2)}, u32[]{:S(2)}) collective-permute-start(bf16[264,1280]{1,0:T(8,128)(2,1)} %get-tuple-element.51), channel_id=1, source_target_pairs={{0,1},{1,2},{2,3},{3,4},{4,5},{5,6},{6,7},{7,0},{8,9},{9,10},{10,1... | collective-permute-start | bytes 2027528 | tf_op jit(solution)/shard_map/ppermute | solution.py:287
  5.4 45.8 %collective-permute-start.2 = (bf16[264,1280]{1,0:T(8,128)(2,1)}, bf16[264,1280]{1,0:T(8,128)(2,1)S(1)}, u32[]{:S(2)}, u32[]{:S(2)}) collective-permute-start(bf16[264,1280]{1,0:T(8,128)(2,1)} %get-tuple-element.48), channel_id=1, source_target_pairs={{0,7},{1,0},{2,1},{3,2},{4,3},{5,4},{6,5},{7,6},{8,15},{9,8},{10,9... | collective-permute-start | bytes 2027528 | tf_op jit(solution)/shard_map/ppermute | solution.py:287
  7.2 122.3 %collective-permute-start = (bf16[264,1280]{1,0:T(8,128)(2,1)}, bf16[264,1280]{1,0:T(8,128)(2,1)S(1)}, u32[]{:S(2)}, u32[]{:S(2)}) collective-permute-start(bf16[264,1280]{1,0:T(8,128)(2,1)} %get-tuple-element.45), channel_id=1, source_target_pairs={{0,4},{1,5},{2,6},{3,7},{4,0},{5,1},{6,2},{7,3},{8,12},{9,13},{10,... | collective-permute-start | bytes 2027528 | tf_op jit(solution)/shard_map/ppermute | solution.py:287
  9.8 119.7 %collective-permute-start.6 = (bf16[264,1280]{1,0:T(8,128)(2,1)}, bf16[264,1280]{1,0:T(8,128)(2,1)S(1)}, u32[]{:S(2)}, u32[]{:S(2)}) collective-permute-start(bf16[264,1280]{1,0:T(8,128)(2,1)} %get-tuple-element.53), channel_id=1, source_target_pairs={{0,3},{1,4},{2,5},{3,6},{4,7},{5,0},{6,1},{7,2},{8,11},{9,12},{10,... | collective-permute-start | bytes 2027528 | tf_op jit(solution)/shard_map/ppermute | solution.py:287
  9.8 124.2 %collective-permute-start.1 = (bf16[264,1280]{1,0:T(8,128)(2,1)}, bf16[264,1280]{1,0:T(8,128)(2,1)S(1)}, u32[]{:S(2)}, u32[]{:S(2)}) collective-permute-start(bf16[264,1280]{1,0:T(8,128)(2,1)} %get-tuple-element.46), channel_id=1, source_target_pairs={{0,5},{1,6},{2,7},{3,0},{4,1},{5,2},{6,3},{7,4},{8,13},{9,14},{10,... | collective-permute-start | bytes 2027528 | tf_op jit(solution)/shard_map/ppermute | solution.py:287
  20.5 0.8 copy-start.1
  21.3 102.4 %collective-permute-start.5 = (bf16[264,1280]{1,0:T(8,128)(2,1)}, bf16[264,1280]{1,0:T(8,128)(2,1)}, u32[]{:S(2)}, u32[]{:S(2)}) collective-permute-start(bf16[264,1280]{1,0:T(8,128)(2,1)} %get-tuple-element.52), channel_id=1, source_target_pairs={{0,2},{1,3},{2,4},{3,5},{4,6},{5,7},{6,0},{7,1},{8,10},{9,11},{10,... | collective-permute-start | bytes 2027528 | tf_op jit(solution)/shard_map/ppermute | solution.py:287
  51.2 76.0 %collective-permute-start.3 = (bf16[264,1280]{1,0:T(8,128)(2,1)}, bf16[264,1280]{1,0:T(8,128)(2,1)S(1)}, u32[]{:S(2)}, u32[]{:S(2)}) collective-permute-start(bf16[264,1280]{1,0:T(8,128)(2,1)} %get-tuple-element.49), channel_id=1, source_target_pairs={{0,6},{1,7},{2,0},{3,1},{4,2},{5,3},{6,4},{7,5},{8,14},{9,15},{10,... | collective-permute-start | bytes 2027528 | tf_op jit(solution)/shard_map/ppermute | solution.py:287
  53.6 1.1 copy-start.2
  54.6 1.1 copy-start.4
  58.1 65.7 %copy-start.3 = (bf16[264,1280]{1,0:T(8,128)(2,1)S(1)}, bf16[264,1280]{1,0:T(8,128)(2,1)}, u32[]{:S(2)}) copy-start(bf16[264,1280]{1,0:T(8,128)(2,1)} %copy-done.1) | copy-start | bytes 2027524
where the time goes:
time: 145 us; the launch traced here: 143 us
  waiting for transfers between devices  67.4 us (46%)
  starting transfers between devices  36.9 us (25%)
  Pallas kernels  32.8 us (23%)
  local copies, waits for them, and re-layouts  5.39 us (4%)
    ppermute x7, waiting for transfers between devices, per_device(): parts[code] = lax.ppermute(message, 'ctx', pairs)  67.4 us
    ppermute x7, starting transfers between devices, per_device(): parts[code] = lax.ppermute(message, 'ctx', pairs)  36.9 us
    pallas_call x6, Pallas kernels, per_device(): pl.pallas_call(functools.partial(local_kernel, width, heads, count, bool(...  18.7 us
    pallas_call x2, Pallas kernels, pack(): pl.pallas_call(functools.partial(pack_kernel, peers, span, width, heads,...  8.65 us
    pallas_call x1, Pallas kernels, per_device(): pl.pallas_call(functools.partial(carry_kernel, width, whole_group), grid=...  5.44 us
    unnamed x12, local copies, waits for them, and re-layouts  3.04 us
  transfers between devices with their start and end apart: 7, of which 2 were waited for; matrix products, arithmetic and copies ran while one was open for 2% of the time, Pallas kernels for 13%

commit v1 on v0

--- a/solution.py
+++ b/solution.py
@@ -277,8 +277,8 @@
 
     codes = [code for code in ORDER if code < peers]
     codes += [code for code in range(1, peers) if code not in codes]
-    parts = dict(zip(codes[:WINDOW], pack(codes[:WINDOW])))
-    parts.update(zip(codes[WINDOW:] + [0], pack(codes[WINDOW:] + [0])))
+    parts = dict(zip(codes[:2], pack(codes[:2])))
+    parts.update(zip(codes[2:] + [0], pack(codes[2:] + [0])))
     for i, code in enumerate(codes):
         pairs = [(j, (j + code) % peers) for j in range(peers)]
         message = parts[code]

time: 145 us -> 143 us (0.986)
  starting transfers between devices: 36.9 us -> 31.8 us
  waiting for transfers between devices: 67.4 us -> 71.3 us
    ppermute x7, starting transfers between devices: 36.9 us -> 31.8 us  [per_device(): parts[code] = lax.ppermute(message, 'ctx', pairs)]
    ppermute x7, waiting for transfers between devices: 67.4 us -> 71.3 us  [per_device(): parts[code] = lax.ppermute(message, 'ctx', pairs)]
  transfers between devices with their start and end apart: 7 -> 7, of which waited for: 2 -> 2; matrix products, arithmetic and copies ran while one was open for 2% -> 2% of each run, Pallas kernels for 13% -> 14%
where the time goes in v1:
time: 143 us; the launch traced here: 142 us
  waiting for transfers between devices  71.3 us (50%)
  Pallas kernels  32.8 us (23%)
  starting transfers between devices  31.8 us (22%)
  local copies, waits for them, and re-layouts  5.41 us (4%)
    ppermute x7, waiting for transfers between devices, per_device(): parts[code] = lax.ppermute(message, 'ctx', pairs)  71.3 us
    ppermute x7, starting transfers between devices, per_device(): parts[code] = lax.ppermute(message, 'ctx', pairs)  31.8 us
    pallas_call x6, Pallas kernels, per_device(): pl.pallas_call(functools.partial(local_kernel, width, heads, count, bool(...  18.7 us
    pallas_call x2, Pallas kernels, pack(): pl.pallas_call(functools.partial(pack_kernel, peers, span, width, heads,...  8.61 us
    pallas_call x1, Pallas kernels, per_device(): pl.pallas_call(functools.partial(carry_kernel, width, whole_group), grid=...  5.44 us
    unnamed x12, local copies, waits for them, and re-layouts  3.05 us
  transfers between devices with their start and end apart: 7, of which 2 were waited for; matrix products, arithmetic and copies ran while one was open for 2% of the time, Pallas kernels for 14%

profile of v1, /device:TPU:12, one launch (start us, length us, event | category | flops | bytes accessed | tf_op | source)
XLA Modules:
  0.0 142.0 jit_solution(16177124859024421831)
XLA Ops:
  0.0 0.0 copy-start
  0.0 0.5 compare_select_fusion.refs_0_
  0.5 0.0 copy-start.5
  0.5 3.6 %pack.3 = (bf16[264,1280]{1,0:T(8,128)(2,1)}, bf16[264,1280]{1,0:T(8,128)(2,1)}) custom-call(s32[8]{0:T(128)} %compare_select_fusion.refs_0_, bf16[256,8192]{1,0:T(8,128)(2,1)} %refs_1_.3, bf16[256,2048]{1,0:T(8,128)(2,1)} %refs_2_.3, f32[256,128]{1,0:T(8,128)} %refs_3_.3, f32[256,128]{1,0:T(8,128)} %refs_4_.3), custom_call_target="tpu_custom_call" | custom-call | bytes 2621440 | tf_op jit(solution)/shard_map/pack/pallas_call | solution.py:260
  4.1 0.1 collective-permute-start.4
  4.2 1.7 %collective-permute-start.2 = (bf16[264,1280]{1,0:T(8,128)(2,1)}, bf16[264,1280]{1,0:T(8,128)(2,1)S(1)}, u32[]{:S(2)}, u32[]{:S(2)}) collective-permute-start(bf16[264,1280]{1,0:T(8,128)(2,1)} %get-tuple-element.48), channel_id=1, source_target_pairs={{0,7},{1,0},{2,1},{3,2},{4,3},{5,4},{6,5},{7,6},{8,15},{9,8},{10,9... | collective-permute-start | bytes 2027528 | tf_op jit(solution)/shard_map/ppermute | solution.py:287
  5.9 5.0 %pack.2 = (bf16[264,1280]{1,0:T(8,128)(2,1)}, bf16[264,1280]{1,0:T(8,128)(2,1)}, bf16[264,1280]{1,0:T(8,128)(2,1)}, bf16[264,1280]{1,0:T(8,128)(2,1)}, bf16[264,...) custom-call(s32[8]{0:T(128)} %compare_select_fusion.refs_0_, bf16[256,8192]{1,0:T(8,128)(2,1)} %refs_1_.3, ...), custom_call_target="tpu_custom_call" | custom-call | bytes 7864320 | tf_op jit(solution)/shard_map/pack/pallas_call | solution.py:260
  11.0 2.7 %collective-permute-start = (bf16[264,1280]{1,0:T(8,128)(2,1)}, bf16[264,1280]{1,0:T(8,128)(2,1)S(1)}, u32[]{:S(2)}, u32[]{:S(2)}) collective-permute-start(bf16[264,1280]{1,0:T(8,128)(2,1)} %get-tuple-element.45), channel_id=1, source_target_pairs={{0,4},{1,5},{2,6},{3,7},{4,0},{5,1},{6,2},{7,3},{8,12},{9,13},{10,... | collective-permute-start | bytes 2027528 | tf_op jit(solution)/shard_map/ppermute | solution.py:287
  13.6 0.0 collective-permute-start.6
  13.6 2.6 %collective-permute-start.1 = (bf16[264,1280]{1,0:T(8,128)(2,1)}, bf16[264,1280]{1,0:T(8,128)(2,1)S(1)}, u32[]{:S(2)}, u32[]{:S(2)}) collective-permute-start(bf16[264,1280]{1,0:T(8,128)(2,1)} %get-tuple-element.46), channel_id=1, source_target_pairs={{0,5},{1,6},{2,7},{3,0},{4,1},{5,2},{6,3},{7,4},{8,13},{9,14},{10,... | collective-permute-start | bytes 2027528 | tf_op jit(solution)/shard_map/ppermute | solution.py:287
  16.3 0.0 copy-done
  16.3 2.9 %collective-permute-done.4.refs_2_.refs_1_ = bf16[264,1280]{1,0:T(8,128)(2,1)S(1)} collective-permute-done((bf16[264,1280]{1,0:T(8,128)(2,1)}, bf16[264,1280]{1,0:T(8,128)(2,1)S(1)}, u32[]{:S(2)}, u32[]{:S(2)}) %collective-permute-start.4) | collective-permute-done | bytes 675872 | tf_op jit(solution)/shard_map/ppermute | solution.py:287
  19.2 0.0 copy-start.1
  19.2 0.9 copy-done.1
  20.1 24.7 %collective-permute-start.5 = (bf16[264,1280]{1,0:T(8,128)(2,1)}, bf16[264,1280]{1,0:T(8,128)(2,1)}, u32[]{:S(2)}, u32[]{:S(2)}) collective-permute-start(bf16[264,1280]{1,0:T(8,128)(2,1)} %get-tuple-element.52), channel_id=1, source_target_pairs={{0,2},{1,3},{2,4},{3,5},{4,6},{5,7},{6,0},{7,1},{8,10},{9,11},{10,... | collective-permute-start | bytes 2027528 | tf_op jit(solution)/shard_map/ppermute | solution.py:287
  44.8 0.0 collective-permute-done.2.refs_1_.refs_2_
  44.9 0.0 collective-permute-start.3
  44.9 0.7 fusion.2
  45.5 0.0 copy-done.5
  45.5 0.1 dynamic_slice.18
  45.6 0.1 broadcast_in_dim.4
  45.7 0.1 broadcast_in_dim_reshape.3.refs_4_.refs_6_
  45.7 0.7 dynamic-slice.3
  46.4 0.7 constant_dynamic-slice_fusion.1
  47.1 0.1 fusion.3
  47.2 0.0 copy-start.2
  47.2 1.1 copy-done.2
  48.3 0.0 copy-start.4
  48.3 1.1 copy-done.4
  49.4 2.3 %local.6 = (bf16[8,256,1024]{2,1,0:T(8,128)(2,1)S(1)}, bf16[8,256,1024]{2,1,0:T(8,128)(2,1)S(1)}, bf16[8,256,128]{2,1,0:T(8,128)(2,1)S(1)}, bf16[8,256,1024]{2,1,0:T(8,128)(2,1)S(1)}, f32[8,4,1024]{2,1,0:T(4,128)S(1)}) custom-call(s32[1]{0:T(128)} %get-tuple-element.87.refs_0_, bf16[264,1280]{1,0:T(8,128)(2,1)S(1)} %copy-done.4, ...), custom_call_target="tpu_custom_call" | custom-call | flops 235929600 | bytes 2621440 | tf_op jit(solution)/shard_map/local/pallas_call | solution.py:322
  51.7 0.0 copy-start.3
  51.7 2.4 %local.7 = (bf16[8,256,1024]{2,1,0:T(8,128)(2,1)S(1)}, bf16[8,256,1024]{2,1,0:T(8,128)(2,1)S(1)}, bf16[8,256,128]{2,1,0:T(8,128)(2,1)S(1)}, bf16[8,256,1024]{2,1,0:T(8,128)(2,1)S(1)}, f32[8,4,1024]{2,1,0:T(4,128)S(1)}) custom-call(s32[1]{0:T(128)} %get-tuple-element.88.refs_0_, ...), custom_call_target="tpu_custom_call", output_to_operand_aliasing={{0}: (5, {}), {1}: (6, {}), {2}: (7, {}), {3}: (8, {}), {4}... | custom-call | flops 235929600 | bytes 2621440 | tf_op jit(solution)/shard_map/local/pallas_call | solution.py:322
  54.1 68.4 %collective-permute-done.5.refs_2_.refs_1_ = bf16[264,1280]{1,0:T(8,128)(2,1)} collective-permute-done((bf16[264,1280]{1,0:T(8,128)(2,1)}, bf16[264,1280]{1,0:T(8,128)(2,1)}, u32[]{:S(2)}, u32[]{:S(2)}) %collective-permute-start.5) | collective-permute-done | bytes 675872 | tf_op jit(solution)/shard_map/ppermute | solution.py:287
  122.5 0.0 copy-done.3
  122.5 3.4 %local.8 = (bf16[8,256,1024]{2,1,0:T(8,128)(2,1)S(1)}, bf16[8,256,1024]{2,1,0:T(8,128)(2,1)S(1)}, bf16[8,256,128]{2,1,0:T(8,128)(2,1)S(1)}, bf16[8,256,1024]{2,1,0:T(8,128)(2,1)S(1)}, f32[8,4,1024]{2,1,0:T(4,128)S(1)}) custom-call(s32[1]{0:T(128)} %get-tuple-element.89.refs_0_, ...), custom_call_target="tpu_custom_call", output_to_operand_aliasing={{0}: (5, {}), {1}: (6, {}), {2}: (7, {}), {3}: (8, {}), {4}... | custom-call | flops 235929600 | bytes 2621440 | tf_op jit(solution)/shard_map/local/pallas_call | solution.py:322
  125.9 0.0 collective-permute-done.3.refs_1_.refs_4_
  125.9 2.3 %local.9 = (bf16[8,256,1024]{2,1,0:T(8,128)(2,1)S(1)}, bf16[8,256,1024]{2,1,0:T(8,128)(2,1)S(1)}, bf16[8,256,128]{2,1,0:T(8,128)(2,1)S(1)}, bf16[8,256,1024]{2,1,0:T(8,128)(2,1)S(1)}, f32[8,4,1024]{2,1,0:T(4,128)S(1)}) custom-call(s32[1]{0:T(128)} %get-tuple-element.90.refs_0_, ...), custom_call_target="tpu_custom_call", output_to_operand_aliasing={{0}: (5, {}), {1}: (6, {}), {2}: (7, {}), {3}: (8, {}), {4}... | custom-call | flops 235929600 | bytes 2621440 | tf_op jit(solution)/shard_map/local/pallas_call | solution.py:322
  128.2 0.0 collective-permute-done.refs_4_.refs_1_
  128.2 0.0 collective-permute-done.6.refs_2_.refs_3_
  128.2 4.5 %local.10 = (bf16[8,256,1024]{2,1,0:T(8,128)(2,1)S(1)}, bf16[8,256,1024]{2,1,0:T(8,128)(2,1)S(1)}, bf16[8,256,128]{2,1,0:T(8,128)(2,1)S(1)}, bf16[8,256,1024]{2,1,0:T(8,128)(2,1)S(1)}, f32[8,4,1024]{2,1,0:T(4,128)S(1)}) custom-call(s32[2]{0:T(128)S(1)} %get-tuple-element.91.refs_0_, ...), custom_call_target="tpu_custom_call", output_to_operand_aliasing={{0}: (7, {}), {1}: (8, {}), {2}: (9, {}), {3}: (10, {}), {4... | custom-call | flops 471859200 | bytes 5242880 | tf_op jit(solution)/shard_map/local/pallas_call | solution.py:322
  132.7 0.0 collective-permute-done.1.refs_2_.refs_3_
  132.7 3.9 %local.11 = (bf16[8,256,1024]{2,1,0:T(8,128)(2,1)S(1)}, bf16[8,256,1024]{2,1,0:T(8,128)(2,1)S(1)}, bf16[8,256,128]{2,1,0:T(8,128)(2,1)S(1)}, bf16[8,256,1024]{2,1,0:T(8,128)(2,1)S(1)}, f32[8,4,1024]{2,1,0:T(4,128)S(1)}) custom-call(s32[2]{0:T(128)S(1)} %get-tuple-element.92.refs_0_, ...), custom_call_target="tpu_custom_call", output_to_operand_aliasing={{0}: (7, {}), {1}: (8, {}), {2}: (9, {}), {3}: (10, {}), {4... | custom-call | flops 471859200 | bytes 5242880 | tf_op jit(solution)/shard_map/local/pallas_call | solution.py:322
  136.6 5.4 %carry.1 = bf16[2048,1024]{1,0:T(8,128)(2,1)} custom-call(bf16[8,256,1024]{2,1,0:T(8,128)(2,1)S(1)} %get-tuple-element.80.refs_0_, bf16[8,256,1024]{2,1,0:T(8,128)(2,1)S(1)} %get-tuple-element.81.refs_1_, bf16[8,256,128]{2,1,0:T(8,128)(2,1)S(1)} %get-tuple-element.82.refs_2_, bf16[8,256,1024]{2,1,0:T(8,128)(2,1)S(1)} %get-tuple-element.83.refs_3_, ...), custom_call_target="tpu_custom_call" | custom-call | flops 629145600 | bytes 16777216 | tf_op jit(solution)/shard_map/carry/pallas_call | solution.py:346
  (3 shorter events, 0.0 us)
Async XLA Ops:
  0.0 16.3 %copy-start = (f32[4,8192]{1,0:T(4,128)S(1)}, f32[4,8192]{1,0:T(4,128)}, u32[]{:S(2)}) copy-start(f32[4,8192]{1,0:T(4,128)} %param.10) | copy-start | bytes 393220
  0.5 45.0 %copy-start.5 = (f32[128]{0:T(128)S(1)}, f32[128]{0:T(128)}, u32[]{:S(2)}) copy-start(f32[128]{0:T(128)} %param.14) | copy-start | bytes 1540
  4.1 15.1 %collective-permute-start.4 = (bf16[264,1280]{1,0:T(8,128)(2,1)}, bf16[264,1280]{1,0:T(8,128)(2,1)S(1)}, u32[]{:S(2)}, u32[]{:S(2)}) collective-permute-start(bf16[264,1280]{1,0:T(8,128)(2,1)} %get-tuple-element.51), channel_id=1, source_target_pairs={{0,1},{1,2},{2,3},{3,4},{4,5},{5,6},{6,7},{7,0},{8,9},{9,10},{10,1... | collective-permute-start | bytes 2027528 | tf_op jit(solution)/shard_map/ppermute | solution.py:287
  4.2 40.7 %collective-permute-start.2 = (bf16[264,1280]{1,0:T(8,128)(2,1)}, bf16[264,1280]{1,0:T(8,128)(2,1)S(1)}, u32[]{:S(2)}, u32[]{:S(2)}) collective-permute-start(bf16[264,1280]{1,0:T(8,128)(2,1)} %get-tuple-element.48), channel_id=1, source_target_pairs={{0,7},{1,0},{2,1},{3,2},{4,3},{5,4},{6,5},{7,6},{8,15},{9,8},{10,9... | collective-permute-start | bytes 2027528 | tf_op jit(solution)/shard_map/ppermute | solution.py:287
  11.0 117.2 %collective-permute-start = (bf16[264,1280]{1,0:T(8,128)(2,1)}, bf16[264,1280]{1,0:T(8,128)(2,1)S(1)}, u32[]{:S(2)}, u32[]{:S(2)}) collective-permute-start(bf16[264,1280]{1,0:T(8,128)(2,1)} %get-tuple-element.45), channel_id=1, source_target_pairs={{0,4},{1,5},{2,6},{3,7},{4,0},{5,1},{6,2},{7,3},{8,12},{9,13},{10,... | collective-permute-start | bytes 2027528 | tf_op jit(solution)/shard_map/ppermute | solution.py:287
  13.6 114.6 %collective-permute-start.6 = (bf16[264,1280]{1,0:T(8,128)(2,1)}, bf16[264,1280]{1,0:T(8,128)(2,1)S(1)}, u32[]{:S(2)}, u32[]{:S(2)}) collective-permute-start(bf16[264,1280]{1,0:T(8,128)(2,1)} %get-tuple-element.53), channel_id=1, source_target_pairs={{0,3},{1,4},{2,5},{3,6},{4,7},{5,0},{6,1},{7,2},{8,11},{9,12},{10,... | collective-permute-start | bytes 2027528 | tf_op jit(solution)/shard_map/ppermute | solution.py:287
  13.6 119.1 %collective-permute-start.1 = (bf16[264,1280]{1,0:T(8,128)(2,1)}, bf16[264,1280]{1,0:T(8,128)(2,1)S(1)}, u32[]{:S(2)}, u32[]{:S(2)}) collective-permute-start(bf16[264,1280]{1,0:T(8,128)(2,1)} %get-tuple-element.46), channel_id=1, source_target_pairs={{0,5},{1,6},{2,7},{3,0},{4,1},{5,2},{6,3},{7,4},{8,13},{9,14},{10,... | collective-permute-start | bytes 2027528 | tf_op jit(solution)/shard_map/ppermute | solution.py:287
  19.2 0.9 copy-start.1
  20.1 102.4 %collective-permute-start.5 = (bf16[264,1280]{1,0:T(8,128)(2,1)}, bf16[264,1280]{1,0:T(8,128)(2,1)}, u32[]{:S(2)}, u32[]{:S(2)}) collective-permute-start(bf16[264,1280]{1,0:T(8,128)(2,1)} %get-tuple-element.52), channel_id=1, source_target_pairs={{0,2},{1,3},{2,4},{3,5},{4,6},{5,7},{6,0},{7,1},{8,10},{9,11},{10,... | collective-permute-start | bytes 2027528 | tf_op jit(solution)/shard_map/ppermute | solution.py:287
  44.9 81.1 %collective-permute-start.3 = (bf16[264,1280]{1,0:T(8,128)(2,1)}, bf16[264,1280]{1,0:T(8,128)(2,1)S(1)}, u32[]{:S(2)}, u32[]{:S(2)}) collective-permute-start(bf16[264,1280]{1,0:T(8,128)(2,1)} %get-tuple-element.49), channel_id=1, source_target_pairs={{0,6},{1,7},{2,0},{3,1},{4,2},{5,3},{6,4},{7,5},{8,14},{9,15},{10,... | collective-permute-start | bytes 2027528 | tf_op jit(solution)/shard_map/ppermute | solution.py:287
  47.2 1.1 copy-start.2
  48.3 1.1 copy-start.4
  51.7 70.8 %copy-start.3 = (bf16[264,1280]{1,0:T(8,128)(2,1)S(1)}, bf16[264,1280]{1,0:T(8,128)(2,1)}, u32[]{:S(2)}) copy-start(bf16[264,1280]{1,0:T(8,128)(2,1)} %copy-done.1) | copy-start | bytes 2027524
